TPU v7x, 32 devices: a whole 2x2x4 slice. The times are simulated.
32 devices in a mesh: groups: 2 (over y), adapter: 4 (over z), tensor: 2 (over x), seq: 2 (over core).
Axes of the slice: x: 2, y: 2, z: 4, core: 2. Of those that a mesh axis runs over, the one named last changes fastest.
Arguments:
- tokens: bfloat16 [2, 6144, 8192], P(None, ('groups', 'adapter', 'seq'), 'tensor'), parts along dimension 1, may hold values from -6 to 6
- token_adapter_index: int32 [2, 6144, 1], P(None, ('groups', 'adapter', 'seq')), parts along dimension 1, may hold values from 0 to 3; in each aligned block of 384 rows (0 to 383, 384 to 767, ..., all dimensions but the last counted through in order) at most 192 rows name the same one
- base_key_weight: bfloat16 [8192, 512], P(('tensor', 'seq')), may hold values from -0.0625 to 0.0625
- lowrank_down_weight: bfloat16 [4, 8192, 64], P('adapter', 'tensor'), may hold values from -0.0625 to 0.0625
- lowrank_up_weight: bfloat16 [4, 64, 512], P('adapter'), may hold values from -0.75 to 0.75
Outputs:
- keys: bfloat16 [2, 6144, 512], P(None, ('groups', 'adapter', 'seq'), 'tensor'), parts along dimension 1
There are 2 independent parts, one for each index of `groups`. A program takes and returns all parts, laid end to end along the dimension named above; an argument that names none is the same for every part. Nothing has to cross between parts.
Inputs may be any that keep to these rules, and one draw needn't show every extreme that they name: `token_adapter_index`: in each micro-batch the 384 tokens of one device (aligned blocks along the token dimension) name one adapter at most 192 times, and in some block an adapter is named exactly 192 times; every adapter is named somewhere.
All inputs are finite; a program needn't handle non-finite values.
Results may differ from a plain program's by a relative error of at most 0.001.
Values may be sent and summed in bfloat16 or wider, within the bound.
A program may use at most 128 MiB of HBM per device.

v0:
```python
import jax
import jax.numpy as jnp
from jax import lax
from jax.sharding import PartitionSpec as P


def place_rows(chosen, adapter_list, capacity):
    micro, row_count = chosen.shape
    onehot = (
        chosen[:, :, None] == jnp.arange(adapter_list, dtype=jnp.int32)[None, None, :]
    ).astype(jnp.int32)
    before = jnp.cumsum(onehot, axis=1) - onehot
    position = jnp.sum(before * onehot, axis=2)
    slots = chosen * capacity + position
    filler = jnp.full((micro, adapter_list * capacity), row_count, jnp.int32)
    batch_index = jnp.arange(micro, dtype=jnp.int32)[:, None]
    row_numbers = jnp.broadcast_to(
        jnp.arange(row_count, dtype=jnp.int32)[None, :], (micro, row_count)
    )
    source_tokens = filler.at[batch_index, slots].set(row_numbers)
    return (slots, source_tokens)


def local(tokens, token_adapter_index, base_key_weight, lowrank_down_weight, lowrank_up_weight):
    micro, tok_rows, part_width = tokens.shape
    key_cols = base_key_weight.shape[1]
    adapter_list = lowrank_down_weight.shape[0] * lax.axis_size("adapter")
    capacity = 2 * tok_rows // adapter_list
    chosen = token_adapter_index[:, :, 0]
    slots, source_tokens = place_rows(chosen, adapter_list, capacity)
    padded = jnp.concatenate([tokens, jnp.zeros((micro, 1, part_width), tokens.dtype)], axis=1)
    buffer = jnp.take_along_axis(padded, source_tokens[:, :, None], axis=1)
    buffer = buffer.reshape(micro, adapter_list, capacity, part_width)
    flat_tokens = tokens.reshape(micro * tok_rows, part_width)
    base_part = jnp.dot(
        flat_tokens,
        lax.all_gather(base_key_weight, "seq", axis=0, tiled=True),
        preferred_element_type=jnp.float32,
    )
    reduced = jnp.einsum(
        "masd,adr->masr",
        lax.all_to_all(buffer, "adapter", split_axis=1, concat_axis=2, tiled=True),
        lowrank_down_weight,
        preferred_element_type=jnp.float32,
    )
    reduced = lax.psum(reduced, "tensor")
    token_portion = key_cols // lax.axis_size("tensor")
    upper_cols = lax.dynamic_slice_in_dim(
        lowrank_up_weight, lax.axis_index("tensor") * token_portion, token_portion, 2
    ).astype(jnp.float32)
    outputs = jnp.einsum("masr,are->mase", reduced, upper_cols, precision=lax.Precision.HIGHEST)
    returned = lax.all_to_all(outputs, "adapter", split_axis=2, concat_axis=1, tiled=True)
    width_now = returned.shape[3]
    flat_out = returned.reshape(micro, adapter_list * capacity, width_now)
    adapter_output = jnp.take_along_axis(flat_out, slots[:, :, None], axis=1).reshape(
        micro * tok_rows, width_now
    )
    summed = lax.psum_scatter(base_part, "tensor", scatter_dimension=1, tiled=True)
    summed = summed + adapter_output
    return summed.reshape(micro, tok_rows, summed.shape[1]).astype(jnp.bfloat16)


def solution(mesh):
    placed = (
        P(None, ("groups", "adapter", "seq"), "tensor"),
        P(None, ("groups", "adapter", "seq"), None),
        P(("tensor", "seq"), None),
        P("adapter", "tensor", None),
        P("adapter", None, None),
    )
    return jax.shard_map(
        local,
        mesh=mesh,
        in_specs=placed,
        out_specs=P(None, ("groups", "adapter", "seq"), "tensor"),
        check_vma=False,
    )
```

profile of v0, /device:TPU:0, one launch (start us, length us, event | category | flops | bytes accessed | tf_op | source)
XLA Modules:
  0.0 530.5 jit_solution(10638255791103009393)
XLA Ops:
  7.4 0.0 copy-start
  7.4 0.7 copy.27
  8.1 0.7 reduce
  8.8 2.4 reduce-window.6
  11.3 0.1 slice.14
  11.4 0.1 copy.14
  11.5 0.1 copy.15
  11.6 0.1 broadcast_add_fusion
  11.7 0.7 and_reduce_fusion
  12.5 36.2 %scatter_fusion = s32[2,768]{1,0:T(2,128)S(1)} fusion(s32[2,768]{1,0:T(2,128)S(1)} %broadcast_in_dim.42, s32[768]{0:T(1024)S(1)} %reshape.88, s32[768]{0:T(1024)S(1)} %reshape.90), kind=kCustom, calls=%fused_computation.2 | custom fusion | bytes 15360 | tf_op jit(solution)/shard_map/scatter | solution.py:20
  48.8 12.7 %copy.17 = bf16[2,384,4096]{2,0,1:T(2,128)(2,1)} copy(bf16[2,384,4096]{2,1,0:T(8,128)(2,1)} %param.5) | data formatting | bytes 12582912 | tf_op args[0]
  61.5 0.1 broadcast_in_dim.45
  61.6 7.2 %concatenate.7 = bf16[2,385,4096]{2,0,1:T(2,128)(2,1)} pad(bf16[2,384,4096]{2,0,1:T(2,128)(2,1)} %copy.17, bf16[]{:T(256)} %constant.47.clone.1), padding=0_0x0_1x0_0 | pad | bytes 12599298 | tf_op jit(solution)/shard_map/concatenate | solution.py:31
  68.7 72.1 %gather_fusion = bf16[1536,4096]{1,0:T(8,128)(2,1)} fusion(bf16[2,385,4096]{2,0,1:T(2,128)(2,1)} %concatenate.7, s32[1536]{0:T(1024)S(1)} %reshape.76), kind=kCustom, calls=%fused_computation | custom fusion | bytes 25178112 | tf_op jit(solution)/shard_map/jit(take_along_axis)/gather | solution.py:32
  140.8 10.8 %copy_select_fusion = bf16[2,4,192,4096]{3,2,0,1:T(8,128)(2,1)} fusion(bf16[2,4,192,4096]{3,2,1,0:T(8,128)(2,1)} %bitcast.40, pred[2,4,192]{2,0,1:T(4,128)(4,1)S(1)} %copy.16), kind=kLoop, calls=%fused_computation.3 | loop fusion | flops 6291456 | bytes 25167360 | tf_op jit(solution)/shard_map/jit(take_along_axis)/select_n | solution.py:32
  151.6 6.3 %all-to-all-start = ((bf16[2,4,192,4096]{3,2,0,1:T(8,128)(2,1)}), bf16[2,4,192,4096]{3,2,0,1:T(8,128)(2,1)}, u32[]{:S(2)}, u32[]{:S(2)}) async-start(bf16[2,4,192,4096]{3,2,0,1:T(8,128)(2,1)} %copy_select_fusion), calls=%async_computation.1 | async-start | bytes 25165824 | tf_op jit(solution)/shard_map/all_to_all | solution.py:42
  158.0 0.0 all-gather.2.cloned.1.call-start
  158.0 0.7 all-gather.2.cloned.1.call-update
  158.7 0.0 all-reduce.3.cloned.1.call-start
  158.7 274.0 %all-to-all-done = bf16[2,4,192,4096]{3,2,0,1:T(8,128)(2,1)} async-done(((bf16[2,4,192,4096]{3,2,0,1:T(8,128)(2,1)}), bf16[2,4,192,4096]{3,2,0,1:T(8,128)(2,1)}, u32[]{:S(2)}, u32[]{:S(2)}) %all-to-all-start) | async-done | bytes 12582944 | tf_op jit(solution)/shard_map/all_to_all | solution.py:42
  432.8 6.3 %copy.19 = bf16[2,4,192,4096]{3,2,1,0:T(8,128)(2,1)S(1)} copy(bf16[2,4,192,4096]{3,2,0,1:T(8,128)(2,1)} %all-to-all-done) | data formatting | bytes 25165824 | tf_op jit(solution)/shard_map/all_to_all | solution.py:42
  439.0 0.0 copy-done
  439.0 4.7 fusion
  443.7 0.0 all-reduce.3.cloned.1.call-update
  443.7 0.0 reduce-scatter.2.cloned.1.call-start
  443.8 0.0 all-gather.2.cloned.1.call-done
  443.8 0.0 copy-start.1
  443.8 8.6 %fusion.14 = f32[768,512]{1,0:T(8,128)} fusion(bf16[768,4096]{1,0:T(8,128)(2,1)} %bitcast.42, bf16[4096,512]{1,0:T(8,128)(2,1)} %all-gather.2.cloned.1.call-done), kind=kOutput, calls=%fused_computation.34 | convolution fusion | flops 3221225472 | bytes 12058624 | tf_op jit(solution)/shard_map/dot_general | solution.py:35
  452.4 0.0 reduce-scatter.2.cloned.1.call-update
  452.4 16.2 %all-reduce.3.cloned.1.call-done = f32[2,768,64]{1,2,0:T(8,128)} async-done(((f32[2,768,64]{1,2,0:T(8,128)}), f32[2,768,64]{1,2,0:T(8,128)}) %all-reduce.3.cloned.1.call-update) | async-done | bytes 393232 | tf_op jit(solution)/shard_map/psum | solution.py:46
  468.6 0.0 copy-done.1
  468.6 1.8 convolution_bitcast_fusion
  470.4 2.1 copy.20
  472.5 4.6 all-to-all-start.1
  477.1 36.8 %all-to-all-done.1 = f32[2,1,768,256]{3,0,1,2:T(2,128)} async-done(((f32[2,1,768,256]{3,0,1,2:T(2,128)}), f32[2,1,768,256]{3,0,1,2:T(2,128)}, u32[]{:S(2)}, u32[]{:S(2)}) %all-to-all-start.1) | async-done | bytes 1572896 | tf_op jit(solution)/shard_map/all_to_all | solution.py:52
  513.9 1.5 copy.26
  515.4 5.5 %gather_fusion.1 = f32[768,256]{1,0:T(8,128)S(1)} fusion(f32[2,768,256]{2,1,0:T(8,128)S(1)} %bitcast.41, s32[768]{0:T(1024)S(1)} %reshape.82), kind=kCustom, calls=%fused_computation.1 | custom fusion | bytes 1579008 | tf_op jit(solution)/shard_map/jit(take_along_axis)/gather | solution.py:55
  520.9 0.0 reduce-scatter.2.cloned.1.call-done
  521.0 2.1 add_convert_fusion
  (17 shorter events, 0.2 us)
Async XLA Ops:
  7.4 431.7 %copy-start = (bf16[1,4096,64]{1,2,0:T(8,128)(2,1)S(1)}, bf16[1,4096,64]{1,2,0:T(8,128)(2,1)}, u32[]{:S(2)}) copy-start(bf16[1,4096,64]{1,2,0:T(8,128)(2,1)} %param.8) | copy-start | bytes 1572868
  151.6 281.1 %all-to-all-start = ((bf16[2,4,192,4096]{3,2,0,1:T(8,128)(2,1)}), bf16[2,4,192,4096]{3,2,0,1:T(8,128)(2,1)}, u32[]{:S(2)}, u32[]{:S(2)}) async-start(bf16[2,4,192,4096]{3,2,0,1:T(8,128)(2,1)} %copy_select_fusion), calls=%async_computation.1 | async-start | bytes 25165824 | tf_op jit(solution)/shard_map/all_to_all | solution.py:42
  158.0 285.8 %all-gather.2.cloned.1.call-start = ((), (), s32[]{:S(2)}) async-start(), calls=%async_computation.3 | async-start | bytes 6291456 | tf_op jit(solution)/shard_map/all_gather | solution.py:37
  158.7 309.9 %all-reduce.3.cloned.1.call-start = ((), (), s32[]{:S(2)}) async-start(), calls=%async_computation.5 | async-start | bytes 786432 | tf_op jit(solution)/shard_map/psum | solution.py:46
  443.7 77.2 %reduce-scatter.2.cloned.1.call-start = ((), (), s32[]{:S(2)}) async-start(), calls=%async_computation.4 | async-start | bytes 2359296 | tf_op jit(solution)/shard_map/reduce_scatter | solution.py:58
  443.8 24.8 %copy-start.1 = (bf16[1,64,512]{2,1,0:T(8,128)(2,1)S(1)}, bf16[1,64,512]{2,1,0:T(8,128)(2,1)}, u32[]{:S(2)}) copy-start(bf16[1,64,512]{2,1,0:T(8,128)(2,1)} %param.9) | copy-start | bytes 196612
  472.5 41.4 %all-to-all-start.1 = ((f32[2,1,768,256]{3,0,1,2:T(2,128)}), f32[2,1,768,256]{3,0,1,2:T(2,128)}, u32[]{:S(2)}, u32[]{:S(2)}) async-start(f32[2,1,768,256]{3,0,1,2:T(2,128)} %copy.20), calls=%async_computation.2 | async-start | bytes 3145728 | tf_op jit(solution)/shard_map/all_to_all | solution.py:52
Sparse Core Ops, SparseCore 0:
  160.4 16.6 all-gather.1
Sparse Core Ops, SparseCore 1:
  443.8 24.7 all-reduce.2
  470.8 25.9 reduce-scatter.1
where the time goes:
time: 533 us; the launch traced here: 530 us
  waiting for transfers between devices  328 us (62%)
  local copies, waits for them, and re-layouts  145 us (27%)
  other arithmetic  16.9 us (3%)
  matrix products  15.1 us (3%)
  between operations  15 us (3%)
  starting transfers between devices  11.1 us (2%)
    all_to_all x1, waiting for transfers between devices, local(): lax.all_to_all(buffer, 'adapter', split_axis=1, concat_axis=2, tiled=True)  274 us
    gather x2, local copies, waits for them, and re-layouts, local(): buffer = jnp.take_along_axis(padded, source_tokens[:, :, None], axis=1)  72.1 us
    all_to_all x1, waiting for transfers between devices, local(): lax.all_to_all(outputs, 'adapter', split_axis=2, concat_axis=1, tiled=True)  36.8 us
    scatter x1, local copies, waits for them, and re-layouts, place_rows(): source_tokens = filler.at[batch_index, slots].set(row_numbers)  36.2 us
    psum x1, waiting for transfers between devices, local(): reduced = lax.psum(reduced, 'tensor')  16.2 us
    unnamed x6, local copies, waits for them, and re-layouts  13.4 us
    select_n x1, other arithmetic, local(): buffer = jnp.take_along_axis(padded, source_tokens[:, :, None], axis=1)  10.8 us
  transfers between devices with their start and end apart: 5, of which 3 were waited for; matrix products, arithmetic and copies ran while one was open for 6% of the time, Pallas kernels for 0%

commit v1 on v0

v1 whole, which is shorter than its diff:
```python
import functools

import jax
import jax.numpy as jnp
from jax import lax
from jax.experimental import pallas as pl
from jax.experimental.pallas import tpu as pltpu
from jax.sharding import PartitionSpec as P

F32 = jnp.float32
BF16 = jnp.bfloat16
MESH = pl.DeviceIdType.MESH


def remote(src, dst, send, recv, device):
    return pltpu.make_async_remote_copy(
        src_ref=src, dst_ref=dst, send_sem=send, recv_sem=recv, device_id=device, device_id_type=MESH
    )


def kernel(
    sizes, chunk,
    idx_ref, x_hbm, w_hbm, d_hbm, u_hbm, o_hbm,
    index_v, x_v, w_v, d_v, u_v, base_send, base_recv, base_own, z_own, z_recv, o_v,
    x_sem, load_sem, out_sem, w_sem, pz_sem, py_sem, pc_sem, uz_sem, uy_sem, uc_sem, base_sem, z_sem,
):
    n_g, n_a, n_t, n_s = sizes
    g, a, t, s = [lax.axis_index(name) for name in ("groups", "adapter", "tensor", "seq")]
    rows, width = x_v.shape
    rank = d_hbm.shape[1]
    n_q = n_g * n_s
    part = rank // n_q
    cols = o_v.shape[1]
    steps = rows // chunk
    w_rows = w_hbm.shape[0]

    def load_x(i):
        at = pl.ds(pl.multiple_of(i * chunk, chunk), chunk)
        return pltpu.make_async_copy(x_hbm.at[at], x_v.at[at], x_sem.at[i])

    own_w = pl.ds(pl.multiple_of(s * w_rows, w_rows), w_rows)
    own_cols = pl.ds(pl.multiple_of(t * cols, cols), cols)
    own_rank = pl.ds(pl.multiple_of(a * rank, rank), rank)
    load_d = pltpu.make_async_copy(d_hbm.at[0], d_v.at[own_rank], load_sem.at[0])
    load_u = pltpu.make_async_copy(u_hbm.at[0, :, own_cols], u_v.at[own_rank], load_sem.at[1])
    load_w = pltpu.make_async_copy(w_hbm, w_v.at[own_w], load_sem.at[2])
    load_d.start()
    load_u.start()
    load_w.start()
    for i in range(steps):
        load_x(i).start()

    barrier = pltpu.get_barrier_semaphore()
    peers = [("groups", g, n_g), ("adapter", a, n_a), ("tensor", t, n_t), ("seq", s, n_s)]
    for name, at, size in peers:
        for j in range(1, size):
            pl.semaphore_signal(
                barrier, inc=1, device_id={name: lax.rem(at + j, size)}, device_id_type=MESH
            )

    for i in range(rows // 128):
        line = jnp.broadcast_to(idx_ref[:, i * 128 : (i + 1) * 128], (128, 128))
        index_v[i * 128 : (i + 1) * 128] = line.T

    load_d.wait()
    load_u.wait()
    pl.semaphore_wait(barrier, sum(size - 1 for _, _, size in peers))

    def send_w(j):
        return remote(
            w_hbm, w_v.at[own_w], w_sem.at[0, j], w_sem.at[1, j], {"seq": lax.rem(s + j, n_s)}
        )

    for j in range(1, n_s):
        send_w(j).start()

    def parts(b, q, sems_p, sems_u, k, device):
        at = pl.ds(pl.multiple_of(b * rank + q * part, part), part)
        p_at, u_at = d_v.at[at], u_v.at[at]
        return (
            remote(p_at, p_at, sems_p.at[0, k], sems_p.at[1, k], device),
            remote(u_at, u_at, sems_u.at[0, k], sems_u.at[1, k], device),
        )

    def along_a(d, source):
        return parts(source, g * n_s + s, pz_sem, uz_sem, d, {"adapter": lax.rem(a + d, n_a)})

    def along_g(d, j, owner):
        b = lax.rem(a + n_a - d, n_a)
        return parts(b, owner * n_s + s, py_sem, uy_sem, d * n_g + j, {"groups": lax.rem(g + j, n_g)})

    def along_s(d, e, j, owner):
        b = lax.rem(a + n_a - d, n_a)
        q = lax.rem(g + n_g - e, n_g) * n_s + owner
        return parts(b, q, pc_sem, uc_sem, (d * n_g + e) * n_s + j, {"seq": lax.rem(s + j, n_s)})

    for d in range(1, n_a):
        for copy in along_a(d, a):
            copy.start()

    load_w.wait()
    for j in range(1, n_s):
        sent = send_w(j)
        other = lax.rem(s + n_s - j, n_s)
        remote(
            w_hbm, w_v.at[pl.ds(pl.multiple_of(other * w_rows, w_rows), w_rows)],
            w_sem.at[0, j], w_sem.at[1, j], {"seq": lax.rem(s + j, n_s)},
        ).wait_recv()
        sent.wait_send()

    def at_rows(i, size=chunk):
        return pl.ds(pl.multiple_of(i * size, size), size)

    def send_base(j, i):
        return remote(
            base_send.at[j - 1, at_rows(i)], base_recv.at[j - 1, at_rows(i)],
            base_sem.at[0, (j - 1) * steps + i], base_sem.at[1, (j - 1) * steps + i],
            {"tensor": lax.rem(t + j, n_t)},
        )

    for j in range(1, n_t):
        their = pl.ds(pl.multiple_of(lax.rem(t + j, n_t) * cols, cols), cols)

        def other_columns(i, _):
            if j == 1:
                load_x(i).wait()
            base_send[j - 1, at_rows(i)] = jnp.dot(
                x_v[at_rows(i)], w_v[:, their], preferred_element_type=F32
            )
            send_base(j, i).start()
            return 0

        lax.fori_loop(0, steps, other_columns, 0)

    for d in range(1, n_a):
        for copy in along_a(d, lax.rem(a + n_a - d, n_a)):
            copy.wait_recv()
        for j in range(1, n_g):
            for copy in along_g(d, j, g):
                copy.start()
        for j in range(1, n_s):
            for copy in along_s(d, 0, j, s):
                copy.start()

    def own_columns(i, _):
        base_own[at_rows(i)] = jnp.dot(
            x_v[at_rows(i)], w_v[:, own_cols], preferred_element_type=F32
        )
        return 0

    lax.fori_loop(0, steps, own_columns, 0)

    for d in range(1, n_a):
        for j in range(1, n_g):
            for copy in along_g(d, j, lax.rem(g + n_g - j, n_g)):
                copy.wait_recv()
            for k in range(1, n_s):
                for copy in along_s(d, j, k, s):
                    copy.start()
    for d in range(1, n_a):
        for e in range(n_g):
            for k in range(1, n_s):
                for copy in along_s(d, e, k, lax.rem(s + n_s - k, n_s)):
                    copy.wait_recv()

    short = chunk // 2

    def send_z(j, i):
        return remote(
            z_own.at[at_rows(i, short)], z_recv.at[j - 1, at_rows(i, short)],
            z_sem.at[0, (j - 1) * steps + i], z_sem.at[1, (j - 1) * steps + i],
            {"tensor": lax.rem(t + j, n_t)},
        )

    def low_rank(i, _):
        index = index_v[at_rows(i)]
        partial = lax.dot_general(
            x_v[at_rows(i)], d_v[...], (((1,), (1,)), ((), ())), preferred_element_type=F32
        )
        lane = lax.broadcasted_iota(jnp.int32, (chunk, 2 * rank), 1)
        is_right = (lane >= rank).astype(jnp.int32)
        total = jnp.zeros((chunk, 2 * rank), F32)
        for pair in range(n_a // 2):
            at = slice(2 * rank * pair, 2 * rank * (pair + 1))
            total += jnp.where(index == 2 * pair + is_right, partial[:, at], 0.0)
        total = total + pltpu.roll(total, rank, 1)
        z_own[at_rows(i, short)] = jnp.where(lane[:short] < rank, total[:short], total[short:])
        for j in range(1, n_t):
            send_z(j, i).start()
        return 0

    lax.fori_loop(0, steps, low_rank, 0)

    def store_out(i):
        return pltpu.make_async_copy(o_v.at[at_rows(i)], o_hbm.at[at_rows(i)], out_sem.at[i])

    def finish(i, _):
        z = z_own[at_rows(i, short)]
        total = base_own[at_rows(i)]
        for j in range(1, n_t):
            send_base(j, i).wait_recv()
            total = total + base_recv[j - 1, at_rows(i)]
        for j in range(1, n_t):
            send_z(j, i).wait_recv()
            z = z + z_recv[j - 1, at_rows(i, short)]
        turned = pltpu.roll(z, rank, 1)
        left = lax.broadcasted_iota(jnp.int32, (short, 2 * rank), 1) < rank
        both = jnp.concatenate([jnp.where(left, z, turned), jnp.where(left, turned, z)], axis=0)
        lane = lax.broadcasted_iota(jnp.int32, (chunk, 2 * rank), 1)
        is_right = (lane >= rank).astype(jnp.int32)
        index = index_v[at_rows(i)]
        spread = jnp.concatenate(
            [jnp.where(index == 2 * pair + is_right, both, 0.0) for pair in range(n_a // 2)], axis=1
        )
        high = spread.astype(BF16)
        low = (spread - high.astype(F32)).astype(BF16)
        total = total + jnp.dot(high, u_v[...], preferred_element_type=F32)
        total = total + jnp.dot(low, u_v[...], preferred_element_type=F32)
        o_v[at_rows(i)] = total.astype(BF16)
        store_out(i).start()
        return 0

    lax.fori_loop(0, steps, finish, 0)

    for d in range(1, n_a):
        for copy in along_a(d, a):
            copy.wait_send()
        for j in range(1, n_g):
            for copy in along_g(d, j, g):
                copy.wait_send()
        for e in range(n_g):
            for k in range(1, n_s):
                for copy in along_s(d, e, k, s):
                    copy.wait_send()
    for i in range(steps):
        for j in range(1, n_t):
            send_base(j, i).wait_send()
            send_z(j, i).wait_send()
        store_out(i).wait()


def local(sizes, tokens, token_adapter_index, base_key_weight, lowrank_down_weight, lowrank_up_weight):
    n_g, n_a, n_t, n_s = sizes
    micro, tok_rows, width = tokens.shape
    rows = micro * tok_rows
    key_cols = base_key_weight.shape[1]
    cols = key_cols // n_t
    rank = lowrank_down_weight.shape[2]
    chunk = rows // 4
    steps = rows // chunk
    any_space = pl.BlockSpec(memory_space=pl.ANY)
    dma = pltpu.SemaphoreType.DMA
    out = pl.pallas_call(
        functools.partial(kernel, sizes, chunk),
        out_shape=jax.ShapeDtypeStruct((rows, cols), BF16),
        in_specs=[pl.BlockSpec(memory_space=pltpu.VMEM)] + [any_space] * 4,
        out_specs=any_space,
        scratch_shapes=[
            pltpu.VMEM((rows, 2 * rank), jnp.int32),
            pltpu.VMEM((rows, width), BF16),
            pltpu.VMEM((width, key_cols), BF16),
            pltpu.VMEM((n_a * rank, width), BF16),
            pltpu.VMEM((n_a * rank, cols), BF16),
            pltpu.VMEM((n_t - 1, rows, cols), F32),
            pltpu.VMEM((n_t - 1, rows, cols), F32),
            pltpu.VMEM((rows, cols), F32),
            pltpu.VMEM((rows // 2, 2 * rank), F32),
            pltpu.VMEM((n_t - 1, rows // 2, 2 * rank), F32),
            pltpu.VMEM((rows, cols), BF16),
            dma((steps,)),
            dma((3,)),
            dma((steps,)),
            dma((2, n_s)),
            dma((2, n_a)),
            dma((2, n_a * n_g)),
            dma((2, n_a * n_g * n_s)),
            dma((2, n_a)),
            dma((2, n_a * n_g)),
            dma((2, n_a * n_g * n_s)),
            dma((2, (n_t - 1) * steps)),
            dma((2, (n_t - 1) * steps)),
        ],
        compiler_params=pltpu.CompilerParams(
            collective_id=0, has_side_effects=True, vmem_limit_bytes=56 * 1024 * 1024
        ),
    )(
        token_adapter_index.reshape(1, rows),
        tokens.reshape(rows, width),
        base_key_weight,
        jnp.swapaxes(lowrank_down_weight, 1, 2),
        lowrank_up_weight,
    )
    return out.reshape(micro, tok_rows, cols)


def solution(mesh):
    sizes = tuple(mesh.shape[name] for name in ("groups", "adapter", "tensor", "seq"))
    placed = (
        P(None, ("groups", "adapter", "seq"), "tensor"),
        P(None, ("groups", "adapter", "seq"), None),
        P(("tensor", "seq"), None),
        P("adapter", "tensor", None),
        P("adapter", None, None),
    )
    return jax.shard_map(
        functools.partial(local, sizes),
        mesh=mesh,
        in_specs=placed,
        out_specs=P(None, ("groups", "adapter", "seq"), "tensor"),
        check_vma=False,
    )
```

time: 533 us -> 38.2 us (0.07)
  waiting for transfers between devices: 328 us -> 0 us
  local copies, waits for them, and re-layouts: 145 us -> 1.77 us
  Pallas kernels: 0 us -> 36.3 us
  other arithmetic: 16.9 us -> 0 us
  matrix products: 15.1 us -> 0 us
  between operations: 15 us -> 0.01 us
  starting transfers between devices: 11.1 us -> 0 us
    all_to_all x2 -> x0, waiting for transfers between devices: 311 us -> none  [the longest x1 274 us: local(): lax.all_to_all(buffer, 'adapter', split_axis=1, concat_axis=2, tiled=True)]
    gather x3 -> x0, local copies, waits for them, and re-layouts: 77.6 us -> none  [the longest x2 72.1 us: local(): buffer = jnp.take_along_axis(padded, source_tokens[:, :, None], axis=1)]
    pallas_call x0 -> x1, Pallas kernels: none -> 36.3 us  [local(): pl.pallas_call(functools.partial(kernel, sizes, chunk), out_shape=jax.Sha...]
    scatter x1 -> x0, local copies, waits for them, and re-layouts: 36.2 us -> none  [place_rows(): source_tokens = filler.at[batch_index, slots].set(row_numbers)]
    psum x1 -> x0, waiting for transfers between devices: 16.2 us -> none  [local(): reduced = lax.psum(reduced, 'tensor')]
    dot_general x3 -> x0, matrix products: 15.1 us -> none  [the longest x1 8.59 us: local(): jnp.dot(flat_tokens, lax.all_gather(base_key_weight, 'seq', axis=0, tiled...]
    unnamed x6 -> x1, local copies, waits for them, and re-layouts: 13.4 us -> 1.77 us
    all_to_all x2 -> x0, starting transfers between devices: 10.9 us -> none  [the longest x1 6.34 us: local(): lax.all_to_all(buffer, 'adapter', split_axis=1, concat_axis=2, tiled=True)]
  transfers between devices with their start and end apart: 5 -> 0, of which waited for: 3 -> 0; matrix products, arithmetic and copies ran while one was open for 6% -> 0% of each run, Pallas kernels for 0% -> 0%
where the time goes in v1:
time: 38.2 us; the launch traced here: 38.1 us
  Pallas kernels  36.3 us (95%)
  local copies, waits for them, and re-layouts  1.77 us (5%)
    pallas_call x1, Pallas kernels, local(): pl.pallas_call(functools.partial(kernel, sizes, chunk), out_shape=jax.Sha...  36.3 us
    unnamed x1, local copies, waits for them, and re-layouts  1.77 us

profile of v1, /device:TPU:0, one launch (start us, length us, event | category | flops | bytes accessed | tf_op | source)
XLA Modules:
  0.0 38.1 jit_solution(3666126602034766320)
XLA Ops:
  0.0 36.3 %shard_map.55 = bf16[768,256]{1,0:T(8,128)(2,1)} custom-call(s32[1,768]{1,0:T(1,128)} %bitcast.7, bf16[768,4096]{1,0:T(8,128)(2,1)} %bitcast.4, bf16[2048,512]{1,0:T(8,128)(2,1)} %w_hbm.1, bf16[1,64,4096]{2,1,0:T(8,128)(2,1)} %bitcast.6, bf16[1,64,512]{2,1,0:T(8,128)(2,1)} %u_hbm.1), custom_call_target="tpu_custom_call" | custom-call | tf_op jit(solution)/shard_map/pallas_call | solution.py:253
  36.3 1.8 %copy.7 = bf16[2,384,256]{2,1,0:T(8,128)(2,1)} copy(bf16[2,384,256]{2,1,0:T(8,128)(2,1)} %bitcast.5) | data formatting | bytes 786432

commit v2 on v1

--- a/solution.py
+++ b/solution.py
@@ -18,29 +18,41 @@
     )
 
 
+def coded(value):
+    top = jnp.maximum(jnp.max(jnp.abs(value), axis=0, keepdims=True), 1e-30)
+    return jnp.round(value * (32767.0 / top)).astype(jnp.int32).astype(jnp.int16), top * (1.0 / 32767.0)
+
+
+def decoded(code, step):
+    return code.astype(jnp.int32).astype(F32) * step
+
+
 def kernel(
     sizes, chunk,
     idx_ref, x_hbm, w_hbm, d_hbm, u_hbm, o_hbm,
-    index_v, x_v, w_v, d_v, u_v, base_send, base_recv, base_own, z_own, z_recv, o_v,
-    x_sem, load_sem, out_sem, w_sem, pz_sem, py_sem, pc_sem, uz_sem, uy_sem, uc_sem, base_sem, z_sem,
+    index_v, x_v, w_v, d_v, turned_v, reduced_v, u_v,
+    base_part, base_send, base_recv, step_send, step_recv, base_own, z_own, z_recv, o_v,
+    x_sem, load_sem, out_sem, w_sem, pz_sem, py_sem, pc_sem, uz_sem, uy_sem, uc_sem, base_sem, step_sem, z_sem,
 ):
     n_g, n_a, n_t, n_s = sizes
     g, a, t, s = [lax.axis_index(name) for name in ("groups", "adapter", "tensor", "seq")]
     rows, width = x_v.shape
     rank = d_hbm.shape[1]
     n_q = n_g * n_s
-    part = rank // n_q
+    part, span = rank // n_q, width // n_q
     cols = o_v.shape[1]
     steps = rows // chunk
     w_rows = w_hbm.shape[0]
 
+    def at_rows(i, size=chunk):
+        return pl.ds(pl.multiple_of(i * size, size), size)
+
     def load_x(i):
-        at = pl.ds(pl.multiple_of(i * chunk, chunk), chunk)
-        return pltpu.make_async_copy(x_hbm.at[at], x_v.at[at], x_sem.at[i])
-
-    own_w = pl.ds(pl.multiple_of(s * w_rows, w_rows), w_rows)
-    own_cols = pl.ds(pl.multiple_of(t * cols, cols), cols)
-    own_rank = pl.ds(pl.multiple_of(a * rank, rank), rank)
+        return pltpu.make_async_copy(x_hbm.at[at_rows(i)], x_v.at[at_rows(i)], x_sem.at[i])
+
+    own_w = at_rows(s, w_rows)
+    own_cols = at_rows(t, cols)
+    own_rank = at_rows(a, rank)
     load_d = pltpu.make_async_copy(d_hbm.at[0], d_v.at[own_rank], load_sem.at[0])
     load_u = pltpu.make_async_copy(u_hbm.at[0, :, own_cols], u_v.at[own_rank], load_sem.at[1])
     load_w = pltpu.make_async_copy(w_hbm, w_v.at[own_w], load_sem.at[2])
@@ -66,17 +78,9 @@
     load_u.wait()
     pl.semaphore_wait(barrier, sum(size - 1 for _, _, size in peers))
 
-    def send_w(j):
-        return remote(
-            w_hbm, w_v.at[own_w], w_sem.at[0, j], w_sem.at[1, j], {"seq": lax.rem(s + j, n_s)}
-        )
-
-    for j in range(1, n_s):
-        send_w(j).start()
-
     def parts(b, q, sems_p, sems_u, k, device):
-        at = pl.ds(pl.multiple_of(b * rank + q * part, part), part)
-        p_at, u_at = d_v.at[at], u_v.at[at]
+        p_at = d_v.at[at_rows(b, rank), at_rows(q, span)]
+        u_at = u_v.at[pl.ds(pl.multiple_of(b * rank + q * part, part), part)]
         return (
             remote(p_at, p_at, sems_p.at[0, k], sems_p.at[1, k], device),
             remote(u_at, u_at, sems_u.at[0, k], sems_u.at[1, k], device),
@@ -94,45 +98,74 @@
         q = lax.rem(g + n_g - e, n_g) * n_s + owner
         return parts(b, q, pc_sem, uc_sem, (d * n_g + e) * n_s + j, {"seq": lax.rem(s + j, n_s)})
 
-    for d in range(1, n_a):
+    near_first = sorted(range(1, n_a), key=lambda d: (min(d, n_a - d), d))
+    for d in near_first:
         for copy in along_a(d, a):
             copy.start()
 
+    def send_w(j, k, owner):
+        at = at_rows(lax.rem(t + k, n_t), cols)
+        return remote(
+            w_hbm.at[:, at], w_v.at[at_rows(owner, w_rows), at],
+            w_sem.at[0, j * n_t + k], w_sem.at[1, j * n_t + k], {"seq": lax.rem(s + j, n_s)},
+        )
+
+    order = list(range(1, n_t)) + [0]
+    for k in order:
+        for j in range(1, n_s):
+            send_w(j, k, s).start()
+
     load_w.wait()
-    for j in range(1, n_s):
-        sent = send_w(j)
-        other = lax.rem(s + n_s - j, n_s)
-        remote(
-            w_hbm, w_v.at[pl.ds(pl.multiple_of(other * w_rows, w_rows), w_rows)],
-            w_sem.at[0, j], w_sem.at[1, j], {"seq": lax.rem(s + j, n_s)},
-        ).wait_recv()
-        sent.wait_send()
-
-    def at_rows(i, size=chunk):
-        return pl.ds(pl.multiple_of(i * size, size), size)
+
+    def own_rows(i, _):
+        load_x(i).wait()
+        for k in range(n_t):
+            base_part[k, at_rows(i)] = jnp.dot(
+                x_v[at_rows(i), own_w], w_v[own_w, at_rows(lax.rem(t + k, n_t), cols)],
+                preferred_element_type=F32,
+            )
+        return 0
+
+    lax.fori_loop(0, steps, own_rows, 0)
+
+    def other_rows(i, k):
+        total = base_part[k, at_rows(i)]
+        for j in range(1, n_s):
+            at = at_rows(lax.rem(s + j, n_s), w_rows)
+            total = total + jnp.dot(
+                x_v[at_rows(i), at], w_v[at, at_rows(lax.rem(t + k, n_t), cols)],
+                preferred_element_type=F32,
+            )
+        return total
 
     def send_base(j, i):
-        return remote(
-            base_send.at[j - 1, at_rows(i)], base_recv.at[j - 1, at_rows(i)],
-            base_sem.at[0, (j - 1) * steps + i], base_sem.at[1, (j - 1) * steps + i],
-            {"tensor": lax.rem(t + j, n_t)},
-        )
-
-    for j in range(1, n_t):
-        their = pl.ds(pl.multiple_of(lax.rem(t + j, n_t) * cols, cols), cols)
+        k = (j - 1) * steps + i
+        device = {"tensor": lax.rem(t + j, n_t)}
+        return (
+            remote(
+                base_send.at[j - 1, at_rows(i)], base_recv.at[j - 1, at_rows(i)],
+                base_sem.at[0, k], base_sem.at[1, k], device,
+            ),
+            remote(
+                step_send.at[k], step_recv.at[k], step_sem.at[0, k], step_sem.at[1, k], device
+            ),
+        )
+
+    for k in range(1, n_t):
+        for j in range(1, n_s):
+            send_w(j, k, lax.rem(s + n_s - j, n_s)).wait_recv()
 
         def other_columns(i, _):
-            if j == 1:
-                load_x(i).wait()
-            base_send[j - 1, at_rows(i)] = jnp.dot(
-                x_v[at_rows(i)], w_v[:, their], preferred_element_type=F32
-            )
-            send_base(j, i).start()
+            code, step = coded(other_rows(i, k))
+            base_send[k - 1, at_rows(i)] = code
+            step_send[(k - 1) * steps + i] = jnp.broadcast_to(step, step_send.shape[1:])
+            for copy in send_base(k, i):
+                copy.start()
             return 0
 
         lax.fori_loop(0, steps, other_columns, 0)
 
-    for d in range(1, n_a):
+    def pass_on(d):
         for copy in along_a(d, lax.rem(a + n_a - d, n_a)):
             copy.wait_recv()
         for j in range(1, n_g):
@@ -142,26 +175,51 @@
             for copy in along_s(d, 0, j, s):
                 copy.start()
 
+    early = len(near_first) * 2 // 3
+    for d in near_first[:early]:
+        pass_on(d)
+
+    for j in range(1, n_s):
+        send_w(j, 0, lax.rem(s + n_s - j, n_s)).wait_recv()
+
     def own_columns(i, _):
-        base_own[at_rows(i)] = jnp.dot(
-            x_v[at_rows(i)], w_v[:, own_cols], preferred_element_type=F32
-        )
+        base_own[at_rows(i)] = other_rows(i, 0)
         return 0
 
     lax.fori_loop(0, steps, own_columns, 0)
 
-    for d in range(1, n_a):
+    for d in near_first[early:]:
+        pass_on(d)
+
+    def reduce_part(q, fresh):
+        at = at_rows(q, span)
+        turned_v[...] = d_v[:, at].T
+
+        def some(i, _):
+            more = jnp.dot(x_v[at_rows(i), at], turned_v[...], preferred_element_type=F32)
+            reduced_v[at_rows(i)] = more if fresh else reduced_v[at_rows(i)] + more
+            return 0
+
+        lax.fori_loop(0, steps, some, 0)
+
+    reduce_part(g * n_s + s, True)
+    for d in near_first:
         for j in range(1, n_g):
             for copy in along_g(d, j, lax.rem(g + n_g - j, n_g)):
                 copy.wait_recv()
             for k in range(1, n_s):
                 for copy in along_s(d, j, k, s):
                     copy.start()
-    for d in range(1, n_a):
-        for e in range(n_g):
-            for k in range(1, n_s):
-                for copy in along_s(d, e, k, lax.rem(s + n_s - k, n_s)):
+    for e in range(n_g):
+        at_g = lax.rem(g + n_g - e, n_g) * n_s
+        if e:
+            reduce_part(at_g + s, False)
+        for k in range(1, n_s):
+            owner = lax.rem(s + n_s - k, n_s)
+            for d in near_first:
+                for copy in along_s(d, e, k, owner):
                     copy.wait_recv()
+            reduce_part(at_g + owner, False)
 
     short = chunk // 2
 
@@ -174,9 +232,7 @@
 
     def low_rank(i, _):
         index = index_v[at_rows(i)]
-        partial = lax.dot_general(
-            x_v[at_rows(i)], d_v[...], (((1,), (1,)), ((), ())), preferred_element_type=F32
-        )
+        partial = reduced_v[at_rows(i)]
         lane = lax.broadcasted_iota(jnp.int32, (chunk, 2 * rank), 1)
         is_right = (lane >= rank).astype(jnp.int32)
         total = jnp.zeros((chunk, 2 * rank), F32)
@@ -198,8 +254,11 @@
         z = z_own[at_rows(i, short)]
         total = base_own[at_rows(i)]
         for j in range(1, n_t):
-            send_base(j, i).wait_recv()
-            total = total + base_recv[j - 1, at_rows(i)]
+            for copy in send_base(j, i):
+                copy.wait_recv()
+            total = total + decoded(
+                base_recv[j - 1, at_rows(i)], step_recv[(j - 1) * steps + i][:1]
+            )
         for j in range(1, n_t):
             send_z(j, i).wait_recv()
             z = z + z_recv[j - 1, at_rows(i, short)]
@@ -222,6 +281,9 @@
 
     lax.fori_loop(0, steps, finish, 0)
 
+    for k in order:
+        for j in range(1, n_s):
+            send_w(j, k, s).wait_send()
     for d in range(1, n_a):
         for copy in along_a(d, a):
             copy.wait_send()
@@ -234,7 +296,8 @@
                     copy.wait_send()
     for i in range(steps):
         for j in range(1, n_t):
-            send_base(j, i).wait_send()
+            for copy in send_base(j, i):
+                copy.wait_send()
             send_z(j, i).wait_send()
         store_out(i).wait()
 
@@ -260,9 +323,14 @@
             pltpu.VMEM((rows, width), BF16),
             pltpu.VMEM((width, key_cols), BF16),
             pltpu.VMEM((n_a * rank, width), BF16),
+            pltpu.VMEM((width // (n_g * n_s), n_a * rank), BF16),
+            pltpu.VMEM((rows, n_a * rank), F32),
             pltpu.VMEM((n_a * rank, cols), BF16),
-            pltpu.VMEM((n_t - 1, rows, cols), F32),
-            pltpu.VMEM((n_t - 1, rows, cols), F32),
+            pltpu.VMEM((n_t, rows, cols), F32),
+            pltpu.VMEM((n_t - 1, rows, cols), jnp.int16),
+            pltpu.VMEM((n_t - 1, rows, cols), jnp.int16),
+            pltpu.VMEM(((n_t - 1) * steps, 8, cols), F32),
+            pltpu.VMEM(((n_t - 1) * steps, 8, cols), F32),
             pltpu.VMEM((rows, cols), F32),
             pltpu.VMEM((rows // 2, 2 * rank), F32),
             pltpu.VMEM((n_t - 1, rows // 2, 2 * rank), F32),
@@ -270,13 +338,14 @@
             dma((steps,)),
             dma((3,)),
             dma((steps,)),
-            dma((2, n_s)),
+            dma((2, n_s * n_t)),
             dma((2, n_a)),
             dma((2, n_a * n_g)),
             dma((2, n_a * n_g * n_s)),
             dma((2, n_a)),
             dma((2, n_a * n_g)),
             dma((2, n_a * n_g * n_s)),
+            dma((2, (n_t - 1) * steps)),
             dma((2, (n_t - 1) * steps)),
             dma((2, (n_t - 1) * steps)),
         ],

time: 38.2 us -> 37.8 us (0.990)
  Pallas kernels: 36.3 us -> 35.9 us
    pallas_call x1, Pallas kernels: 36.3 us -> 35.9 us  [local(): pl.pallas_call(functools.partial(kernel, sizes, chunk), out_shape=jax.Sha...]
where the time goes in v2:
time: 37.8 us; the launch traced here: 37.7 us
  Pallas kernels  35.9 us (95%)
  local copies, waits for them, and re-layouts  1.77 us (5%)
    pallas_call x1, Pallas kernels, local(): pl.pallas_call(functools.partial(kernel, sizes, chunk), out_shape=jax.Sha...  35.9 us
    unnamed x1, local copies, waits for them, and re-layouts  1.77 us

profile of v2, /device:TPU:0, one launch (start us, length us, event | category | flops | bytes accessed | tf_op | source)
XLA Modules:
  0.0 37.7 jit_solution(1493618779974922503)
XLA Ops:
  0.0 35.9 %shard_map.55 = bf16[768,256]{1,0:T(8,128)(2,1)} custom-call(s32[1,768]{1,0:T(1,128)} %bitcast.7, bf16[768,4096]{1,0:T(8,128)(2,1)} %bitcast.4, bf16[2048,512]{1,0:T(8,128)(2,1)} %w_hbm.1, bf16[1,64,4096]{2,1,0:T(8,128)(2,1)} %bitcast.6, bf16[1,64,512]{2,1,0:T(8,128)(2,1)} %u_hbm.1), custom_call_target="tpu_custom_call" | custom-call | tf_op jit(solution)/shard_map/pallas_call | solution.py:316
  35.9 1.8 %copy.7 = bf16[2,384,256]{2,1,0:T(8,128)(2,1)} copy(bf16[2,384,256]{2,1,0:T(8,128)(2,1)} %bitcast.5) | data formatting | bytes 786432

commit v3 on v2

--- a/solution.py
+++ b/solution.py
@@ -31,15 +31,15 @@
     sizes, chunk,
     idx_ref, x_hbm, w_hbm, d_hbm, u_hbm, o_hbm,
     index_v, x_v, w_v, d_v, turned_v, reduced_v, u_v,
-    base_part, base_send, base_recv, step_send, step_recv, base_own, z_own, z_recv, o_v,
-    x_sem, load_sem, out_sem, w_sem, pz_sem, py_sem, pc_sem, uz_sem, uy_sem, uc_sem, base_sem, step_sem, z_sem,
+    base_part, base_send, base_recv, step_send, step_recv, base_own, z_own, z_send, z_recv, z_step_send, z_step_recv, o_v,
+    x_sem, load_sem, out_sem, w_sem, pz_sem, py_sem, pc_sem, uz_sem, base_sem, step_sem, z_sem, z_step_sem,
 ):
     n_g, n_a, n_t, n_s = sizes
     g, a, t, s = [lax.axis_index(name) for name in ("groups", "adapter", "tensor", "seq")]
     rows, width = x_v.shape
     rank = d_hbm.shape[1]
     n_q = n_g * n_s
-    part, span = rank // n_q, width // n_q
+    span = width // n_q
     cols = o_v.shape[1]
     steps = rows // chunk
     w_rows = w_hbm.shape[0]
@@ -59,8 +59,6 @@
     load_d.start()
     load_u.start()
     load_w.start()
-    for i in range(steps):
-        load_x(i).start()
 
     barrier = pltpu.get_barrier_semaphore()
     peers = [("groups", g, n_g), ("adapter", a, n_a), ("tensor", t, n_t), ("seq", s, n_s)]
@@ -78,30 +76,34 @@
     load_u.wait()
     pl.semaphore_wait(barrier, sum(size - 1 for _, _, size in peers))
 
-    def parts(b, q, sems_p, sems_u, k, device):
+    def parts(b, q, sems_p, k, device):
         p_at = d_v.at[at_rows(b, rank), at_rows(q, span)]
-        u_at = u_v.at[pl.ds(pl.multiple_of(b * rank + q * part, part), part)]
-        return (
-            remote(p_at, p_at, sems_p.at[0, k], sems_p.at[1, k], device),
-            remote(u_at, u_at, sems_u.at[0, k], sems_u.at[1, k], device),
-        )
+        return (remote(p_at, p_at, sems_p.at[0, k], sems_p.at[1, k], device),)
+
+    def send_u(d, source):
+        at = u_v.at[at_rows(source, rank)]
+        return remote(at, at, uz_sem.at[0, d], uz_sem.at[1, d], {"adapter": lax.rem(a + d, n_a)})
 
     def along_a(d, source):
-        return parts(source, g * n_s + s, pz_sem, uz_sem, d, {"adapter": lax.rem(a + d, n_a)})
+        return parts(source, g * n_s + s, pz_sem, d, {"adapter": lax.rem(a + d, n_a)})
 
     def along_g(d, j, owner):
         b = lax.rem(a + n_a - d, n_a)
-        return parts(b, owner * n_s + s, py_sem, uy_sem, d * n_g + j, {"groups": lax.rem(g + j, n_g)})
+        return parts(b, owner * n_s + s, py_sem, d * n_g + j, {"groups": lax.rem(g + j, n_g)})
 
     def along_s(d, e, j, owner):
         b = lax.rem(a + n_a - d, n_a)
         q = lax.rem(g + n_g - e, n_g) * n_s + owner
-        return parts(b, q, pc_sem, uc_sem, (d * n_g + e) * n_s + j, {"seq": lax.rem(s + j, n_s)})
+        return parts(b, q, pc_sem, (d * n_g + e) * n_s + j, {"seq": lax.rem(s + j, n_s)})
 
     near_first = sorted(range(1, n_a), key=lambda d: (min(d, n_a - d), d))
     for d in near_first:
         for copy in along_a(d, a):
             copy.start()
+    for d in near_first:
+        send_u(d, a).start()
+    for i in range(steps):
+        load_x(i).start()
 
     def send_w(j, k, owner):
         at = at_rows(lax.rem(t + k, n_t), cols)
@@ -224,10 +226,16 @@
     short = chunk // 2
 
     def send_z(j, i):
-        return remote(
-            z_own.at[at_rows(i, short)], z_recv.at[j - 1, at_rows(i, short)],
-            z_sem.at[0, (j - 1) * steps + i], z_sem.at[1, (j - 1) * steps + i],
-            {"tensor": lax.rem(t + j, n_t)},
+        k = (j - 1) * steps + i
+        device = {"tensor": lax.rem(t + j, n_t)}
+        return (
+            remote(
+                z_send.at[at_rows(i, short)], z_recv.at[j - 1, at_rows(i, short)],
+                z_sem.at[0, k], z_sem.at[1, k], device,
+            ),
+            remote(
+                z_step_send.at[i], z_step_recv.at[k], z_step_sem.at[0, k], z_step_sem.at[1, k], device
+            ),
         )
 
     def low_rank(i, _):
@@ -240,12 +248,20 @@
             at = slice(2 * rank * pair, 2 * rank * (pair + 1))
             total += jnp.where(index == 2 * pair + is_right, partial[:, at], 0.0)
         total = total + pltpu.roll(total, rank, 1)
-        z_own[at_rows(i, short)] = jnp.where(lane[:short] < rank, total[:short], total[short:])
+        total = jnp.where(lane[:short] < rank, total[:short], total[short:])
+        z_own[at_rows(i, short)] = total
+        code, step = coded(total)
+        z_send[at_rows(i, short)] = code
+        z_step_send[i] = jnp.broadcast_to(step, z_step_send.shape[1:])
         for j in range(1, n_t):
-            send_z(j, i).start()
+            for copy in send_z(j, i):
+                copy.start()
         return 0
 
     lax.fori_loop(0, steps, low_rank, 0)
+
+    for d in near_first:
+        send_u(d, lax.rem(a + n_a - d, n_a)).wait_recv()
 
     def store_out(i):
         return pltpu.make_async_copy(o_v.at[at_rows(i)], o_hbm.at[at_rows(i)], out_sem.at[i])
@@ -260,8 +276,9 @@
                 base_recv[j - 1, at_rows(i)], step_recv[(j - 1) * steps + i][:1]
             )
         for j in range(1, n_t):
-            send_z(j, i).wait_recv()
-            z = z + z_recv[j - 1, at_rows(i, short)]
+            for copy in send_z(j, i):
+                copy.wait_recv()
+            z = z + decoded(z_recv[j - 1, at_rows(i, short)], z_step_recv[(j - 1) * steps + i][:1])
         turned = pltpu.roll(z, rank, 1)
         left = lax.broadcasted_iota(jnp.int32, (short, 2 * rank), 1) < rank
         both = jnp.concatenate([jnp.where(left, z, turned), jnp.where(left, turned, z)], axis=0)
@@ -281,6 +298,8 @@
 
     lax.fori_loop(0, steps, finish, 0)
 
+    for d in near_first:
+        send_u(d, a).wait_send()
     for k in order:
         for j in range(1, n_s):
             send_w(j, k, s).wait_send()
@@ -298,7 +317,8 @@
         for j in range(1, n_t):
             for copy in send_base(j, i):
                 copy.wait_send()
-            send_z(j, i).wait_send()
+            for copy in send_z(j, i):
+                copy.wait_send()
         store_out(i).wait()
 
 
@@ -309,7 +329,7 @@
     key_cols = base_key_weight.shape[1]
     cols = key_cols // n_t
     rank = lowrank_down_weight.shape[2]
-    chunk = rows // 4
+    chunk = rows // 2
     steps = rows // chunk
     any_space = pl.BlockSpec(memory_space=pl.ANY)
     dma = pltpu.SemaphoreType.DMA
@@ -333,7 +353,10 @@
             pltpu.VMEM(((n_t - 1) * steps, 8, cols), F32),
             pltpu.VMEM((rows, cols), F32),
             pltpu.VMEM((rows // 2, 2 * rank), F32),
-            pltpu.VMEM((n_t - 1, rows // 2, 2 * rank), F32),
+            pltpu.VMEM((rows // 2, 2 * rank), jnp.int16),
+            pltpu.VMEM((n_t - 1, rows // 2, 2 * rank), jnp.int16),
+            pltpu.VMEM((steps, 8, 2 * rank), F32),
+            pltpu.VMEM(((n_t - 1) * steps, 8, 2 * rank), F32),
             pltpu.VMEM((rows, cols), BF16),
             dma((steps,)),
             dma((3,)),
@@ -343,8 +366,7 @@
             dma((2, n_a * n_g)),
             dma((2, n_a * n_g * n_s)),
             dma((2, n_a)),
-            dma((2, n_a * n_g)),
-            dma((2, n_a * n_g * n_s)),
+            dma((2, (n_t - 1) * steps)),
             dma((2, (n_t - 1) * steps)),
             dma((2, (n_t - 1) * steps)),
             dma((2, (n_t - 1) * steps)),

time: 37.8 us -> 35.5 us (0.939)
  Pallas kernels: 35.9 us -> 33.5 us
    pallas_call x1, Pallas kernels: 35.9 us -> 33.5 us  [local(): pl.pallas_call(functools.partial(kernel, sizes, chunk), out_shape=jax.Sha...]
where the time goes in v3:
time: 35.5 us; the launch traced here: 35.3 us
  Pallas kernels  33.5 us (94%)
  local copies, waits for them, and re-layouts  1.77 us (5%)
    pallas_call x1, Pallas kernels, local(): pl.pallas_call(functools.partial(kernel, sizes, chunk), out_shape=jax.Sha...  33.5 us
    unnamed x1, local copies, waits for them, and re-layouts  1.77 us

profile of v3, /device:TPU:0, one launch (start us, length us, event | category | flops | bytes accessed | tf_op | source)
XLA Modules:
  0.0 35.3 jit_solution(226441011705450291)
XLA Ops:
  0.0 33.5 %shard_map.55 = bf16[768,256]{1,0:T(8,128)(2,1)} custom-call(s32[1,768]{1,0:T(1,128)} %bitcast.7, bf16[768,4096]{1,0:T(8,128)(2,1)} %bitcast.4, bf16[2048,512]{1,0:T(8,128)(2,1)} %w_hbm.1, bf16[1,64,4096]{2,1,0:T(8,128)(2,1)} %bitcast.6, bf16[1,64,512]{2,1,0:T(8,128)(2,1)} %u_hbm.1), custom_call_target="tpu_custom_call" | custom-call | tf_op jit(solution)/shard_map/pallas_call | solution.py:336
  33.5 1.8 %copy.7 = bf16[2,384,256]{2,1,0:T(8,128)(2,1)} copy(bf16[2,384,256]{2,1,0:T(8,128)(2,1)} %bitcast.5) | data formatting | bytes 786432

commit v4 on v3

--- a/solution.py
+++ b/solution.py
@@ -30,7 +30,7 @@
 def kernel(
     sizes, chunk,
     idx_ref, x_hbm, w_hbm, d_hbm, u_hbm, o_hbm,
-    index_v, x_v, w_v, d_v, turned_v, reduced_v, u_v,
+    index_v, x_v, w_v, d_v, reduced_v, u_v,
     base_part, base_send, base_recv, step_send, step_recv, base_own, z_own, z_send, z_recv, z_step_send, z_step_recv, o_v,
     x_sem, load_sem, out_sem, w_sem, pz_sem, py_sem, pc_sem, uz_sem, base_sem, step_sem, z_sem, z_step_sem,
 ):
@@ -192,36 +192,6 @@
 
     for d in near_first[early:]:
         pass_on(d)
-
-    def reduce_part(q, fresh):
-        at = at_rows(q, span)
-        turned_v[...] = d_v[:, at].T
-
-        def some(i, _):
-            more = jnp.dot(x_v[at_rows(i), at], turned_v[...], preferred_element_type=F32)
-            reduced_v[at_rows(i)] = more if fresh else reduced_v[at_rows(i)] + more
-            return 0
-
-        lax.fori_loop(0, steps, some, 0)
-
-    reduce_part(g * n_s + s, True)
-    for d in near_first:
-        for j in range(1, n_g):
-            for copy in along_g(d, j, lax.rem(g + n_g - j, n_g)):
-                copy.wait_recv()
-            for k in range(1, n_s):
-                for copy in along_s(d, j, k, s):
-                    copy.start()
-    for e in range(n_g):
-        at_g = lax.rem(g + n_g - e, n_g) * n_s
-        if e:
-            reduce_part(at_g + s, False)
-        for k in range(1, n_s):
-            owner = lax.rem(s + n_s - k, n_s)
-            for d in near_first:
-                for copy in along_s(d, e, k, owner):
-                    copy.wait_recv()
-            reduce_part(at_g + owner, False)
 
     short = chunk // 2
 
@@ -258,7 +228,39 @@
                 copy.start()
         return 0
 
-    lax.fori_loop(0, steps, low_rank, 0)
+    def reduce_part(q, fresh, last=False):
+        at = at_rows(q, span)
+
+        def some(i, _):
+            more = lax.dot_general(
+                x_v[at_rows(i), at], d_v[:, at], (((1,), (1,)), ((), ())), preferred_element_type=F32
+            )
+            reduced_v[at_rows(i)] = more if fresh else reduced_v[at_rows(i)] + more
+            if last:
+                low_rank(i, 0)
+            return 0
+
+        lax.fori_loop(0, steps, some, 0)
+
+    reduce_part(g * n_s + s, True)
+    for d in near_first:
+        for j in range(1, n_g):
+            for copy in along_g(d, j, lax.rem(g + n_g - j, n_g)):
+                copy.wait_recv()
+            for k in range(1, n_s):
+                for copy in along_s(d, j, k, s):
+                    copy.start()
+    for e in range(n_g):
+        at_g = lax.rem(g + n_g - e, n_g) * n_s
+        if e:
+            reduce_part(at_g + s, False)
+        for k in range(1, n_s):
+            owner = lax.rem(s + n_s - k, n_s)
+            for d in near_first:
+                for copy in along_s(d, e, k, owner):
+                    copy.wait_recv()
+            reduce_part(at_g + owner, False, e == n_g - 1 and k == n_s - 1)
+
 
     for d in near_first:
         send_u(d, lax.rem(a + n_a - d, n_a)).wait_recv()
@@ -343,7 +345,6 @@
             pltpu.VMEM((rows, width), BF16),
             pltpu.VMEM((width, key_cols), BF16),
             pltpu.VMEM((n_a * rank, width), BF16),
-            pltpu.VMEM((width // (n_g * n_s), n_a * rank), BF16),
             pltpu.VMEM((rows, n_a * rank), F32),
             pltpu.VMEM((n_a * rank, cols), BF16),
             pltpu.VMEM((n_t, rows, cols), F32),

time: 35.5 us -> 34.8 us (0.980)
  Pallas kernels: 33.5 us -> 32.9 us
    pallas_call x1, Pallas kernels: 33.5 us -> 32.9 us  [local(): pl.pallas_call(functools.partial(kernel, sizes, chunk), out_shape=jax.Sha...]
where the time goes in v4:
time: 34.8 us; the launch traced here: 34.6 us
  Pallas kernels  32.9 us (95%)
  local copies, waits for them, and re-layouts  1.77 us (5%)
    pallas_call x1, Pallas kernels, local(): pl.pallas_call(functools.partial(kernel, sizes, chunk), out_shape=jax.Sha...  32.9 us
    unnamed x1, local copies, waits for them, and re-layouts  1.77 us

profile of v4, /device:TPU:0, one launch (start us, length us, event | category | flops | bytes accessed | tf_op | source)
XLA Modules:
  0.0 34.6 jit_solution(6965785676634160308)
XLA Ops:
  0.0 32.9 %shard_map.55 = bf16[768,256]{1,0:T(8,128)(2,1)} custom-call(s32[1,768]{1,0:T(1,128)} %bitcast.7, bf16[768,4096]{1,0:T(8,128)(2,1)} %bitcast.4, bf16[2048,512]{1,0:T(8,128)(2,1)} %w_hbm.1, bf16[1,64,4096]{2,1,0:T(8,128)(2,1)} %bitcast.6, bf16[1,64,512]{2,1,0:T(8,128)(2,1)} %u_hbm.1), custom_call_target="tpu_custom_call" | custom-call | tf_op jit(solution)/shard_map/pallas_call | solution.py:338
  32.9 1.8 %copy.7 = bf16[2,384,256]{2,1,0:T(8,128)(2,1)} copy(bf16[2,384,256]{2,1,0:T(8,128)(2,1)} %bitcast.5) | data formatting | bytes 786432

commit v5 on v4

--- a/solution.py
+++ b/solution.py
@@ -96,11 +96,11 @@
         q = lax.rem(g + n_g - e, n_g) * n_s + owner
         return parts(b, q, pc_sem, (d * n_g + e) * n_s + j, {"seq": lax.rem(s + j, n_s)})
 
-    near_first = sorted(range(1, n_a), key=lambda d: (min(d, n_a - d), d))
-    for d in near_first:
+    far_first = sorted(range(1, n_a), key=lambda d: (-min(d, n_a - d), d))
+    for d in far_first:
         for copy in along_a(d, a):
             copy.start()
-    for d in near_first:
+    for d in far_first:
         send_u(d, a).start()
     for i in range(steps):
         load_x(i).start()
@@ -177,8 +177,8 @@
             for copy in along_s(d, 0, j, s):
                 copy.start()
 
-    early = len(near_first) * 2 // 3
-    for d in near_first[:early]:
+    early = len(far_first) * 2 // 3
+    for d in far_first[:early]:
         pass_on(d)
 
     for j in range(1, n_s):
@@ -190,7 +190,7 @@
 
     lax.fori_loop(0, steps, own_columns, 0)
 
-    for d in near_first[early:]:
+    for d in far_first[early:]:
         pass_on(d)
 
     short = chunk // 2
@@ -243,7 +243,7 @@
         lax.fori_loop(0, steps, some, 0)
 
     reduce_part(g * n_s + s, True)
-    for d in near_first:
+    for d in far_first:
         for j in range(1, n_g):
             for copy in along_g(d, j, lax.rem(g + n_g - j, n_g)):
                 copy.wait_recv()
@@ -256,13 +256,13 @@
             reduce_part(at_g + s, False)
         for k in range(1, n_s):
             owner = lax.rem(s + n_s - k, n_s)
-            for d in near_first:
+            for d in far_first:
                 for copy in along_s(d, e, k, owner):
                     copy.wait_recv()
             reduce_part(at_g + owner, False, e == n_g - 1 and k == n_s - 1)
 
 
-    for d in near_first:
+    for d in far_first:
         send_u(d, lax.rem(a + n_a - d, n_a)).wait_recv()
 
     def store_out(i):
@@ -300,7 +300,7 @@
 
     lax.fori_loop(0, steps, finish, 0)
 
-    for d in near_first:
+    for d in far_first:
         send_u(d, a).wait_send()
     for k in order:
         for j in range(1, n_s):

time: 34.8 us -> 35.5 us (1.020)
  Pallas kernels: 32.9 us -> 33.6 us
    pallas_call x1, Pallas kernels: 32.9 us -> 33.6 us  [local(): pl.pallas_call(functools.partial(kernel, sizes, chunk), out_shape=jax.Sha...]
where the time goes in v5:
time: 35.5 us; the launch traced here: 35.3 us
  Pallas kernels  33.6 us (95%)
  local copies, waits for them, and re-layouts  1.77 us (5%)
    pallas_call x1, Pallas kernels, local(): pl.pallas_call(functools.partial(kernel, sizes, chunk), out_shape=jax.Sha...  33.6 us
    unnamed x1, local copies, waits for them, and re-layouts  1.77 us

profile of v5, /device:TPU:0, one launch (start us, length us, event | category | flops | bytes accessed | tf_op | source)
XLA Modules:
  0.0 35.3 jit_solution(5302441798190140993)
XLA Ops:
  0.0 33.6 %shard_map.55 = bf16[768,256]{1,0:T(8,128)(2,1)} custom-call(s32[1,768]{1,0:T(1,128)} %bitcast.7, bf16[768,4096]{1,0:T(8,128)(2,1)} %bitcast.4, bf16[2048,512]{1,0:T(8,128)(2,1)} %w_hbm.1, bf16[1,64,4096]{2,1,0:T(8,128)(2,1)} %bitcast.6, bf16[1,64,512]{2,1,0:T(8,128)(2,1)} %u_hbm.1), custom_call_target="tpu_custom_call" | custom-call | tf_op jit(solution)/shard_map/pallas_call | solution.py:338
  33.6 1.8 %copy.7 = bf16[2,384,256]{2,1,0:T(8,128)(2,1)} copy(bf16[2,384,256]{2,1,0:T(8,128)(2,1)} %bitcast.5) | data formatting | bytes 786432
